TPU v7x, 32 devices: a whole 2x2x4 slice. The times are simulated.
32 devices in a mesh: groups: 2 (over y), users: 4 (over z), hours: 4 (over x, core).
Axes of the slice: x: 2, y: 2, z: 4, core: 2. Of those that a mesh axis runs over, the one named last changes fastest.
Arguments:
- activity: bfloat16 [16384, 8192], P(('groups', 'users'), 'hours'), parts along dimension 0, may hold values from -6 to 6
- cohort: int32 [16384], P(('groups', 'users')), parts along dimension 0, may hold values from 0 to 15
- tap_table: float32 [16, 9], replicated, may hold values from 0.02 to 0.4
- sketch: bfloat16 [8192, 64], P('hours'), may hold values from -0.0625 to 0.0625
Outputs:
- basis: float32 [16384, 64], P(('groups', 'users', 'hours')), parts along dimension 0
- triangle: float32 [128, 64], P('groups'), parts along dimension 0
There are 2 independent parts, one for each index of `groups`. A program takes and returns all parts, laid end to end along the dimension named above; an argument that names none is the same for every part. Nothing has to cross between parts.
All inputs are finite; a program needn't handle non-finite values.
Results may differ from a plain program's by a relative error of at most 0.003.
Values may be sent and summed in bfloat16 or wider, within the bound.
A program may use at most 64 MiB of HBM per device.

v0:
```python
import math
import jax
import jax.numpy as jnp
from jax import lax
from jax.sharding import PartitionSpec as P

TAPS = 9


def with_halo(block, sides, width):
    for axis, dim in sides:
        count = lax.axis_size(axis)
        forward = [(i, i + 1) for i in range(count - 1)]
        backward = [(target, source) for source, target in forward]
        low = lax.ppermute(
            lax.slice_in_dim(block, block.shape[dim] - width, None, axis=dim), axis, forward
        )
        high = lax.ppermute(lax.slice_in_dim(block, 0, width, axis=dim), axis, backward)
        block = jnp.concatenate([low, block, high], axis=dim)
    return block


def partner_2(value, axis, distance):
    mask = 2**distance
    pairs = [(source, source ^ mask) for source in range(lax.axis_size(axis))]
    return lax.ppermute(value, axis, pairs)


def per_device(activity, cohort, tap_table, sketch):
    rows = activity.shape[0]
    width = activity.shape[1]
    reach = (TAPS - 1) // 2
    padded = with_halo(activity, (("hours", 1),), reach)
    onehot = (cohort[:, None] == jnp.arange(tap_table.shape[0], dtype=jnp.int32)[None, :]).astype(
        jnp.float32
    )
    taps = jnp.dot(onehot, tap_table, precision=lax.Precision.HIGHEST)
    share = rows // lax.axis_size("hours")
    total = jnp.zeros((rows, width), jnp.float32)
    for step in range(TAPS):
        total = total + taps[:, step : step + 1] * padded[:, step : step + width].astype(
            jnp.float32
        )
    smoothed = total.astype(jnp.bfloat16)
    summed = lax.psum(jnp.dot(smoothed, sketch, preferred_element_type=jnp.float32), "hours")
    local = lax.dynamic_slice_in_dim(summed, lax.axis_index("hours") * share, share, 0)
    gram = jnp.dot(local.T, local, precision=lax.Precision.HIGHEST)
    lower = jnp.linalg.cholesky(gram)
    levels = lax.axis_size(("users", "hours")).bit_length() - 1
    for level in range(levels):
        partner = partner_2(lower, ("users", "hours"), level)
        joined = jnp.dot(lower, lower.T, precision=lax.Precision.HIGHEST) + jnp.dot(
            partner, partner.T, precision=lax.Precision.HIGHEST
        )
        lower = jnp.linalg.cholesky(joined)
    basis = lax.linalg.triangular_solve(lower, local, left_side=False, lower=True, transpose_a=True)
    scale = 1.0 / math.sqrt(rows * lax.axis_size("users"))
    triangle = lower.T * jnp.float32(scale)
    return (basis, triangle)


def solution(mesh):
    return jax.shard_map(
        per_device,
        mesh=mesh,
        in_specs=(P(("groups", "users"), "hours"), P(("groups", "users")), P(), P("hours", None)),
        out_specs=(P(("groups", "users", "hours"), None), P("groups", None)),
        check_vma=False,
    )
```

profile of v0, /device:TPU:0, one launch (start us, length us, event | category | flops | bytes accessed | tf_op | source)
XLA Modules:
  0.0 174.9 jit_solution(3421940850101160094)
XLA Ops:
  7.2 1.5 fusion.27
  8.7 2.4 %collective-permute-start = (bf16[2048,4]{1,0:T(8,128)(2,1)S(1)}, bf16[2048,4]{1,0:T(8,128)(2,1)S(1)}, u32[]{:S(2)}, u32[]{:S(2)}) collective-permute-start(bf16[2048,4]{1,0:T(8,128)(2,1)S(1)} %get-tuple-element.6), channel_id=1, source_target_pairs={{0,1},{1,2},{2,3},{4,5},{5,6},{6,7},{8,9},{9,10},{10,11},{12,13},{... | collective-permute-start | bytes 49160 | tf_op jit(solution)/shard_map/ppermute | solution.py:15
  11.1 1.3 collective-permute-start.1
  12.4 8.3 %constant_dynamic-update-slice_fusion.1 = bf16[2048,2052]{1,0:T(8,128)(2,1)} fusion(bf16[2048,2048]{1,0:T(8,128)(2,1)} %param.5), kind=kLoop, calls=%fused_computation.51 | loop fusion | bytes 16777216
  20.7 0.9 fusion.4
  21.8 0.9 constant_dynamic-update-slice_fusion
  22.7 47.5 %fusion.3 = f32[2048,64]{0,1:T(8,128)} fusion(bf16[2048,64]{0,1:T(8,128)(2,1)S(1)} %copy-done, bf16[2048,2048]{1,0:T(8,128)(2,1)} %param.5, bf16[2048,4]{1,0:T(8,128)(2,1)S(1)} %collective-permute-done, bf16[2048,2052]{1,0:T(8,128)(2,1)} %constant_dynamic-update-slice_fusion, f32[2048]{0:T(1024)S(1)} %bitcast.55, f32[2048]{0:T(1024)S(1)} %bitcast.56, ...), kind=kOutput, calls=%fused_computation.9 | convolution fusion | flops 700448768 | bytes 42819584 | tf_op jit(solution)/shard_map/dot_general | solution.py:45
  70.2 37.9 %all-reduce.2.cloned.1.call-done = f32[2048,64]{0,1:T(8,128)} async-done(((f32[2048,64]{0,1:T(8,128)}), f32[2048,64]{0,1:T(8,128)}) %all-reduce.2.cloned.1.call-update) | async-done | bytes 524304 | tf_op jit(solution)/shard_map/psum | solution.py:45
  108.1 1.2 fusion.8
  109.4 5.8 %cholesky.89 = f32[64,64]{1,0:T(8,128)S(1)} custom-call(f32[64,64]{1,0:T(8,128)S(1)} %fusion.15), custom_call_target="Cholesky" | custom-call | tf_op jit(solution)/shard_map/jit(cholesky)/cholesky | solution.py:48
  115.3 0.6 compare_reduce_fusion.4
  115.9 0.7 select_select_fusion.4
  116.9 1.0 collective-permute-done.2
  118.2 5.8 %cholesky.100 = f32[64,64]{1,0:T(8,128)S(1)} custom-call(f32[64,64]{1,0:T(8,128)S(1)} %fusion.14), custom_call_target="Cholesky" | custom-call | tf_op jit(solution)/shard_map/jit(cholesky)/cholesky | solution.py:55
  124.0 0.6 compare_reduce_fusion.3
  124.7 0.7 select_select_fusion.3
  125.7 3.6 %collective-permute-done.3 = f32[64,64]{1,0:T(8,128)S(1)} collective-permute-done((f32[64,64]{1,0:T(8,128)S(1)}, f32[64,64]{1,0:T(8,128)S(1)}, u32[]{:S(2)}, u32[]{:S(2)}) %collective-permute-start.3) | collective-permute-done | bytes 16416 | tf_op jit(solution)/shard_map/ppermute | solution.py:26
  129.6 5.8 %cholesky.111 = f32[64,64]{1,0:T(8,128)S(1)} custom-call(f32[64,64]{1,0:T(8,128)S(1)} %fusion.13), custom_call_target="Cholesky" | custom-call | tf_op jit(solution)/shard_map/jit(cholesky)/cholesky | solution.py:55
  136.1 0.7 select_select_fusion.2
  136.8 1.5 collective-permute-start.4
  138.5 2.2 %collective-permute-done.4 = f32[64,64]{1,0:T(8,128)S(1)} collective-permute-done((f32[64,64]{1,0:T(8,128)S(1)}, f32[64,64]{1,0:T(8,128)S(1)}, u32[]{:S(2)}, u32[]{:S(2)}) %collective-permute-start.4) | collective-permute-done | bytes 16416 | tf_op jit(solution)/shard_map/ppermute | solution.py:26
  141.1 5.8 %cholesky.122 = f32[64,64]{1,0:T(8,128)S(1)} custom-call(f32[64,64]{1,0:T(8,128)S(1)} %fusion.12), custom_call_target="Cholesky" | custom-call | tf_op jit(solution)/shard_map/jit(cholesky)/cholesky | solution.py:55
  147.0 0.6 compare_reduce_fusion.1
  147.6 0.7 select_select_fusion.1
  148.3 2.5 %collective-permute-start.5 = (f32[64,64]{1,0:T(8,128)S(1)}, f32[64,64]{1,0:T(8,128)S(1)}, u32[]{:S(2)}, u32[]{:S(2)}) collective-permute-start(f32[64,64]{1,0:T(8,128)S(1)} %select_select_fusion.1), channel_id=1, source_target_pairs={{0,8},{1,9},{2,10},{3,11},{4,12},{5,13},{6,14},{7,15},{8,0},{9,1},... | collective-permute-start | bytes 49160 | tf_op jit(solution)/shard_map/ppermute | solution.py:26
  150.9 2.2 %collective-permute-done.5 = f32[64,64]{1,0:T(8,128)S(1)} collective-permute-done((f32[64,64]{1,0:T(8,128)S(1)}, f32[64,64]{1,0:T(8,128)S(1)}, u32[]{:S(2)}, u32[]{:S(2)}) %collective-permute-start.5) | collective-permute-done | bytes 16416 | tf_op jit(solution)/shard_map/ppermute | solution.py:26
  153.4 5.8 %cholesky.133 = f32[64,64]{1,0:T(8,128)S(1)} custom-call(f32[64,64]{1,0:T(8,128)S(1)} %fusion.11), custom_call_target="Cholesky" | custom-call | tf_op jit(solution)/shard_map/jit(cholesky)/cholesky | solution.py:55
  159.3 0.6 compare_reduce_fusion
  160.0 0.7 multiply_bitcast_fusion
  160.6 4.9 %custom-call.5 = f32[1,64,64]{1,2,0:T(8,128)S(1)} custom-call(f32[1,64,64]{2,1,0:T(8,128)S(1)} %get-tuple-element.17), custom_call_target="InvertDiagBlocksLowerTriangular" | custom-call | tf_op jit(solution)/shard_map/triangular_solve | solution.py:56
  165.5 0.7 copy.19
  166.2 1.9 %fusion.6 = f32[512,64]{0,1:T(8,128)} fusion(f32[2048,64]{0,1:T(8,128)} %all-reduce.2.cloned.1.call-done, s32[]{:T(128)S(6)} %select_n.6, f32[1,64,64]{1,2,0:T(8,128)S(1)} %custom-call.5), kind=kOutput, calls=%fused_computation.17 | convolution fusion | flops 25165824 | bytes 278532 | tf_op jit(solution)/shard_map/triangular_solve | solution.py:56
  (37 shorter events, 3.1 us)
Async XLA Ops:
  7.2 15.5 %copy-start = (bf16[2048,64]{0,1:T(8,128)(2,1)S(1)}, bf16[2048,64]{0,1:T(8,128)(2,1)}, u32[]{:S(2)}) copy-start(bf16[2048,64]{0,1:T(8,128)(2,1)} %param.8) | copy-start | bytes 786436
  7.2 100.9 %all-reduce.2.cloned.1.call-start = ((), (), s32[]{:S(2)}) async-start(), calls=%async_computation | async-start | bytes 1048576 | tf_op jit(solution)/shard_map/psum | solution.py:45
  8.7 12.1 %copy-start.1 = (f32[16,9]{1,0:T(8,128)S(1)}, f32[16,9]{1,0:T(8,128)}, u32[]{:S(2)}) copy-start(f32[16,9]{1,0:T(8,128)} %param.7) | copy-start | bytes 1732
  8.7 12.1 %copy-start.2 = (s32[2048]{0:T(1024)S(1)}, s32[2048]{0:T(1024)}, u32[]{:S(2)}) copy-start(s32[2048]{0:T(1024)} %param.6) | copy-start | bytes 24580
  8.7 14.0 %collective-permute-start = (bf16[2048,4]{1,0:T(8,128)(2,1)S(1)}, bf16[2048,4]{1,0:T(8,128)(2,1)S(1)}, u32[]{:S(2)}, u32[]{:S(2)}) collective-permute-start(bf16[2048,4]{1,0:T(8,128)(2,1)S(1)} %get-tuple-element.6), channel_id=1, source_target_pairs={{0,1},{1,2},{2,3},{4,5},{5,6},{6,7},{8,9},{9,10},{10,11},{12,13},{... | collective-permute-start | bytes 49160 | tf_op jit(solution)/shard_map/ppermute | solution.py:15
  11.1 10.7 %collective-permute-start.1 = (bf16[2048,4]{1,0:T(8,128)(2,1)S(1)}, bf16[2048,4]{1,0:T(8,128)(2,1)S(1)}, u32[]{:S(2)}, u32[]{:S(2)}) collective-permute-start(bf16[2048,4]{1,0:T(8,128)(2,1)S(1)} %get-tuple-element.5), channel_id=1, source_target_pairs={{1,0},{2,1},{3,2},{5,4},{6,5},{7,6},{9,8},{10,9},{11,10},{13,12},{... | collective-permute-start | bytes 49160 | tf_op jit(solution)/shard_map/ppermute | solution.py:18
  116.6 1.3 collective-permute-start.2
  125.4 4.0 %collective-permute-start.3 = (f32[64,64]{1,0:T(8,128)S(1)}, f32[64,64]{1,0:T(8,128)S(1)}, u32[]{:S(2)}, u32[]{:S(2)}) collective-permute-start(f32[64,64]{1,0:T(8,128)S(1)} %select_select_fusion.3), channel_id=1, source_target_pairs={{0,2},{1,3},{2,0},{3,1},{4,6},{5,7},{6,4},{7,5},{8,10},{9,11},{10,... | collective-permute-start | bytes 49160 | tf_op jit(solution)/shard_map/ppermute | solution.py:26
  136.8 4.0 %collective-permute-start.4 = (f32[64,64]{1,0:T(8,128)S(1)}, f32[64,64]{1,0:T(8,128)S(1)}, u32[]{:S(2)}, u32[]{:S(2)}) collective-permute-start(f32[64,64]{1,0:T(8,128)S(1)} %select_select_fusion.2), channel_id=1, source_target_pairs={{0,4},{1,5},{2,6},{3,7},{4,0},{5,1},{6,2},{7,3},{8,12},{9,13},{10,... | collective-permute-start | bytes 49160 | tf_op jit(solution)/shard_map/ppermute | solution.py:26
  148.3 4.9 %collective-permute-start.5 = (f32[64,64]{1,0:T(8,128)S(1)}, f32[64,64]{1,0:T(8,128)S(1)}, u32[]{:S(2)}, u32[]{:S(2)}) collective-permute-start(f32[64,64]{1,0:T(8,128)S(1)} %select_select_fusion.1), channel_id=1, source_target_pairs={{0,8},{1,9},{2,10},{3,11},{4,12},{5,13},{6,14},{7,15},{8,0},{9,1},... | collective-permute-start | bytes 49160 | tf_op jit(solution)/shard_map/ppermute | solution.py:26
Sparse Core Ops, SparseCore 0:
  70.3 37.7 all-reduce.1
where the time goes:
time: 175 us
  matrix products  53 us (30%)
  waiting for transfers between devices  47 us (27%)
  other arithmetic  40.8 us (23%)
  between operations  14.3 us (8%)
  local copies, waits for them, and re-layouts  11.9 us (7%)
  starting transfers between devices  8 us (5%)
    dot_general x1, matrix products, per_device(): jnp.dot(smoothed, sketch, preferred_element_type=jnp.float32)  47.5 us
    psum x1, waiting for transfers between devices, per_device(): lax.psum(jnp.dot(smoothed, sketch, preferred_element_type=jnp.float32), '...  37.9 us
    another operation x12, other arithmetic, per_device(): lower = jnp.linalg.cholesky(joined)  26.1 us
    unnamed x8, local copies, waits for them, and re-layouts  9.07 us
    ppermute x4, waiting for transfers between devices, partner_2(): return lax.ppermute(value, axis, pairs)  9.06 us
    another operation x3, other arithmetic, per_device(): lower = jnp.linalg.cholesky(gram)  6.52 us
    another operation x1, other arithmetic, per_device(): lax.linalg.triangular_solve(lower, local, left_side=False, lower=True, tr...  4.9 us
    ppermute x4, starting transfers between devices, partner_2(): return lax.ppermute(value, axis, pairs)  4.28 us
  transfers between devices with their start and end apart: 7, of which 5 were waited for; matrix products, arithmetic and copies ran while one was open for 6% of the time, Pallas kernels for 0%

commit v1 on v0

--- a/solution.py
+++ b/solution.py
@@ -42,7 +42,11 @@
             jnp.float32
         )
     smoothed = total.astype(jnp.bfloat16)
-    summed = lax.psum(jnp.dot(smoothed, sketch, preferred_element_type=jnp.float32), "hours")
+
+    def pass_waves(m, device_axis):
+        return lax.all_gather(m, device_axis).sum(axis=0)
+
+    summed = pass_waves(jnp.dot(smoothed, sketch, preferred_element_type=jnp.float32), "hours")
     local = lax.dynamic_slice_in_dim(summed, lax.axis_index("hours") * share, share, 0)
     gram = jnp.dot(local.T, local, precision=lax.Precision.HIGHEST)
     lower = jnp.linalg.cholesky(gram)

time: 175 us -> 167 us (0.954)
  waiting for transfers between devices: 47 us -> 36 us
  local copies, waits for them, and re-layouts: 11.9 us -> 14.7 us
  matrix products: 53 us -> 51.2 us
    psum x1 -> x0, waiting for transfers between devices: 37.9 us -> none  [per_device(): lax.psum(jnp.dot(smoothed, sketch, preferred_element_type=jnp.float32), '...]
    all_gather x0 -> x1, waiting for transfers between devices: none -> 27.3 us  [pass_waves(): return lax.all_gather(m, device_axis).sum(axis=0)]
    all_gather x0 -> x1, local copies, waits for them, and re-layouts: none -> 2.85 us  [pass_waves(): return lax.all_gather(m, device_axis).sum(axis=0)]
  transfers between devices with their start and end apart: 7 -> 7, of which waited for: 5 -> 5; matrix products, arithmetic and copies ran while one was open for 6% -> 7% of each run, Pallas kernels for 0% -> 0%
where the time goes in v1:
time: 167 us
  matrix products  51.2 us (31%)
  other arithmetic  42.1 us (25%)
  waiting for transfers between devices  36 us (22%)
  local copies, waits for them, and re-layouts  14.7 us (9%)
  between operations  14.3 us (9%)
  starting transfers between devices  8.42 us (5%)
    dot_general x1, matrix products, per_device(): jnp.dot(smoothed, sketch, preferred_element_type=jnp.float32)  47.5 us
    all_gather x1, waiting for transfers between devices, pass_waves(): return lax.all_gather(m, device_axis).sum(axis=0)  27.3 us
    another operation x12, other arithmetic, per_device(): lower = jnp.linalg.cholesky(joined)  26.1 us
    unnamed x8, local copies, waits for them, and re-layouts  9.05 us
    ppermute x4, waiting for transfers between devices, partner_2(): return lax.ppermute(value, axis, pairs)  8.64 us
    another operation x3, other arithmetic, per_device(): lower = jnp.linalg.cholesky(gram)  6.52 us
    another operation x1, other arithmetic, per_device(): lax.linalg.triangular_solve(lower, local, left_side=False, lower=True, tr...  4.9 us
    ppermute x4, starting transfers between devices, partner_2(): return lax.ppermute(value, axis, pairs)  4.7 us
  transfers between devices with their start and end apart: 7, of which 5 were waited for; matrix products, arithmetic and copies ran while one was open for 7% of the time, Pallas kernels for 0%

profile of v1, /device:TPU:0, one launch (start us, length us, event | category | flops | bytes accessed | tf_op | source)
XLA Modules:
  0.0 166.7 jit_solution(2018655122681251722)
XLA Ops:
  7.2 1.5 fusion.27
  8.7 2.4 %collective-permute-start = (bf16[2048,4]{1,0:T(8,128)(2,1)S(1)}, bf16[2048,4]{1,0:T(8,128)(2,1)S(1)}, u32[]{:S(2)}, u32[]{:S(2)}) collective-permute-start(bf16[2048,4]{1,0:T(8,128)(2,1)S(1)} %get-tuple-element.8), channel_id=1, source_target_pairs={{0,1},{1,2},{2,3},{4,5},{5,6},{6,7},{8,9},{9,10},{10,11},{12,13},{... | collective-permute-start | bytes 49160 | tf_op jit(solution)/shard_map/ppermute | solution.py:15
  11.1 1.3 collective-permute-start.1
  12.4 8.3 %constant_dynamic-update-slice_fusion.1 = bf16[2048,2052]{1,0:T(8,128)(2,1)} fusion(bf16[2048,2048]{1,0:T(8,128)(2,1)} %param.5), kind=kLoop, calls=%fused_computation.51 | loop fusion | bytes 16777216
  20.7 0.9 fusion.4
  21.8 0.9 constant_dynamic-update-slice_fusion
  22.7 47.5 %fusion.3 = f32[2048,64]{0,1:T(8,128)} fusion(bf16[2048,64]{0,1:T(8,128)(2,1)S(1)} %copy-done, bf16[2048,2048]{1,0:T(8,128)(2,1)} %param.5, bf16[2048,4]{1,0:T(8,128)(2,1)S(1)} %collective-permute-done, bf16[2048,2052]{1,0:T(8,128)(2,1)} %constant_dynamic-update-slice_fusion, f32[2048]{0:T(1024)S(1)} %bitcast.57, f32[2048]{0:T(1024)S(1)} %bitcast.58, ...), kind=kOutput, calls=%fused_computation.9 | convolution fusion | flops 700448768 | bytes 42819584 | tf_op jit(solution)/shard_map/dot_general | solution.py:49
  70.2 27.3 %all-gather.3.cloned.1.call-done = f32[8192,64]{0,1:T(8,128)} async-done(((f32[2048,64]{0,1:T(8,128)}), f32[8192,64]{0,1:T(8,128)}) %all-gather.3.cloned.1.call-update) | async-done | bytes 2097168 | tf_op jit(solution)/shard_map/all_gather | solution.py:47
  97.5 2.9 %reshape.13 = f32[4,2048,64]{1,0,2:T(4,128)S(1)} reshape(f32[8192,64]{0,1:T(8,128)} %all-gather.3.cloned.1.call-done) | data formatting | bytes 4194304 | tf_op jit(solution)/shard_map/all_gather | solution.py:47
  100.4 1.3 reduce_sum.9
  102.1 5.8 %cholesky.89 = f32[64,64]{1,0:T(8,128)S(1)} custom-call(f32[64,64]{1,0:T(8,128)S(1)} %fusion.15), custom_call_target="Cholesky" | custom-call | tf_op jit(solution)/shard_map/jit(cholesky)/cholesky | solution.py:52
  108.6 0.7 select_select_fusion.4
  109.8 0.8 collective-permute-done.2
  110.8 5.8 %cholesky.100 = f32[64,64]{1,0:T(8,128)S(1)} custom-call(f32[64,64]{1,0:T(8,128)S(1)} %fusion.14), custom_call_target="Cholesky" | custom-call | tf_op jit(solution)/shard_map/jit(cholesky)/cholesky | solution.py:59
  116.7 0.6 compare_reduce_fusion.3
  117.3 0.7 select_select_fusion.3
  118.6 3.4 %collective-permute-done.3 = f32[64,64]{1,0:T(8,128)S(1)} collective-permute-done((f32[64,64]{1,0:T(8,128)S(1)}, f32[64,64]{1,0:T(8,128)S(1)}, u32[]{:S(2)}, u32[]{:S(2)}) %collective-permute-start.3) | collective-permute-done | bytes 16416 | tf_op jit(solution)/shard_map/ppermute | solution.py:26
  122.3 5.8 %cholesky.111 = f32[64,64]{1,0:T(8,128)S(1)} custom-call(f32[64,64]{1,0:T(8,128)S(1)} %fusion.13), custom_call_target="Cholesky" | custom-call | tf_op jit(solution)/shard_map/jit(cholesky)/cholesky | solution.py:59
  128.8 0.7 select_select_fusion.2
  129.5 1.5 collective-permute-start.4
  131.2 2.2 %collective-permute-done.4 = f32[64,64]{1,0:T(8,128)S(1)} collective-permute-done((f32[64,64]{1,0:T(8,128)S(1)}, f32[64,64]{1,0:T(8,128)S(1)}, u32[]{:S(2)}, u32[]{:S(2)}) %collective-permute-start.4) | collective-permute-done | bytes 16416 | tf_op jit(solution)/shard_map/ppermute | solution.py:26
  133.7 5.8 %cholesky.122 = f32[64,64]{1,0:T(8,128)S(1)} custom-call(f32[64,64]{1,0:T(8,128)S(1)} %fusion.12), custom_call_target="Cholesky" | custom-call | tf_op jit(solution)/shard_map/jit(cholesky)/cholesky | solution.py:59
  139.6 0.6 compare_reduce_fusion.1
  140.2 0.7 select_select_fusion.1
  140.9 2.5 %collective-permute-start.5 = (f32[64,64]{1,0:T(8,128)S(1)}, f32[64,64]{1,0:T(8,128)S(1)}, u32[]{:S(2)}, u32[]{:S(2)}) collective-permute-start(f32[64,64]{1,0:T(8,128)S(1)} %select_select_fusion.1), channel_id=1, source_target_pairs={{0,8},{1,9},{2,10},{3,11},{4,12},{5,13},{6,14},{7,15},{8,0},{9,1},... | collective-permute-start | bytes 49160 | tf_op jit(solution)/shard_map/ppermute | solution.py:26
  143.6 2.2 %collective-permute-done.5 = f32[64,64]{1,0:T(8,128)S(1)} collective-permute-done((f32[64,64]{1,0:T(8,128)S(1)}, f32[64,64]{1,0:T(8,128)S(1)}, u32[]{:S(2)}, u32[]{:S(2)}) %collective-permute-start.5) | collective-permute-done | bytes 16416 | tf_op jit(solution)/shard_map/ppermute | solution.py:26
  146.1 5.8 %cholesky.133 = f32[64,64]{1,0:T(8,128)S(1)} custom-call(f32[64,64]{1,0:T(8,128)S(1)} %fusion.11), custom_call_target="Cholesky" | custom-call | tf_op jit(solution)/shard_map/jit(cholesky)/cholesky | solution.py:59
  152.0 0.6 compare_reduce_fusion
  152.6 0.7 multiply_bitcast_fusion
  153.3 4.9 %custom-call.5 = f32[1,64,64]{1,2,0:T(8,128)S(1)} custom-call(f32[1,64,64]{2,1,0:T(8,128)S(1)} %get-tuple-element.19), custom_call_target="InvertDiagBlocksLowerTriangular" | custom-call | tf_op jit(solution)/shard_map/triangular_solve | solution.py:60
  158.2 1.0 fusion.6
  159.2 0.7 copy.33
  (39 shorter events, 4.4 us)
Async XLA Ops:
  7.2 15.5 %copy-start = (bf16[2048,64]{0,1:T(8,128)(2,1)S(1)}, bf16[2048,64]{0,1:T(8,128)(2,1)}, u32[]{:S(2)}) copy-start(bf16[2048,64]{0,1:T(8,128)(2,1)} %param.8) | copy-start | bytes 786436
  7.2 90.3 %all-gather.3.cloned.1.call-start = ((), (), s32[]{:S(2)}) async-start(), calls=%async_computation | async-start | bytes 2621440 | tf_op jit(solution)/shard_map/all_gather | solution.py:47
  8.7 12.1 %copy-start.1 = (f32[16,9]{1,0:T(8,128)S(1)}, f32[16,9]{1,0:T(8,128)}, u32[]{:S(2)}) copy-start(f32[16,9]{1,0:T(8,128)} %param.7) | copy-start | bytes 1732
  8.7 12.1 %copy-start.2 = (s32[2048]{0:T(1024)S(1)}, s32[2048]{0:T(1024)}, u32[]{:S(2)}) copy-start(s32[2048]{0:T(1024)} %param.6) | copy-start | bytes 24580
  8.7 14.0 %collective-permute-start = (bf16[2048,4]{1,0:T(8,128)(2,1)S(1)}, bf16[2048,4]{1,0:T(8,128)(2,1)S(1)}, u32[]{:S(2)}, u32[]{:S(2)}) collective-permute-start(bf16[2048,4]{1,0:T(8,128)(2,1)S(1)} %get-tuple-element.8), channel_id=1, source_target_pairs={{0,1},{1,2},{2,3},{4,5},{5,6},{6,7},{8,9},{9,10},{10,11},{12,13},{... | collective-permute-start | bytes 49160 | tf_op jit(solution)/shard_map/ppermute | solution.py:15
  11.1 10.7 %collective-permute-start.1 = (bf16[2048,4]{1,0:T(8,128)(2,1)S(1)}, bf16[2048,4]{1,0:T(8,128)(2,1)S(1)}, u32[]{:S(2)}, u32[]{:S(2)}) collective-permute-start(bf16[2048,4]{1,0:T(8,128)(2,1)S(1)} %get-tuple-element.7), channel_id=1, source_target_pairs={{1,0},{2,1},{3,2},{5,4},{6,5},{7,6},{9,8},{10,9},{11,10},{13,12},{... | collective-permute-start | bytes 49160 | tf_op jit(solution)/shard_map/ppermute | solution.py:18
  109.3 1.3 collective-permute-start.2
  118.0 4.0 %collective-permute-start.3 = (f32[64,64]{1,0:T(8,128)S(1)}, f32[64,64]{1,0:T(8,128)S(1)}, u32[]{:S(2)}, u32[]{:S(2)}) collective-permute-start(f32[64,64]{1,0:T(8,128)S(1)} %select_select_fusion.3), channel_id=1, source_target_pairs={{0,2},{1,3},{2,0},{3,1},{4,6},{5,7},{6,4},{7,5},{8,10},{9,11},{10,... | collective-permute-start | bytes 49160 | tf_op jit(solution)/shard_map/ppermute | solution.py:26
  129.5 4.0 %collective-permute-start.4 = (f32[64,64]{1,0:T(8,128)S(1)}, f32[64,64]{1,0:T(8,128)S(1)}, u32[]{:S(2)}, u32[]{:S(2)}) collective-permute-start(f32[64,64]{1,0:T(8,128)S(1)} %select_select_fusion.2), channel_id=1, source_target_pairs={{0,4},{1,5},{2,6},{3,7},{4,0},{5,1},{6,2},{7,3},{8,12},{9,13},{10,... | collective-permute-start | bytes 49160 | tf_op jit(solution)/shard_map/ppermute | solution.py:26
  140.9 4.9 %collective-permute-start.5 = (f32[64,64]{1,0:T(8,128)S(1)}, f32[64,64]{1,0:T(8,128)S(1)}, u32[]{:S(2)}, u32[]{:S(2)}) collective-permute-start(f32[64,64]{1,0:T(8,128)S(1)} %select_select_fusion.1), channel_id=1, source_target_pairs={{0,8},{1,9},{2,10},{3,11},{4,12},{5,13},{6,14},{7,15},{8,0},{9,1},... | collective-permute-start | bytes 49160 | tf_op jit(solution)/shard_map/ppermute | solution.py:26
Sparse Core Ops, SparseCore 0:
  70.3 27.1 all-gather.2
